TPU v7x, 32 devices: a whole 2x2x4 slice. The times are simulated.
32 devices in a mesh: group: 2 (over y), tensor: 4 (over z), job: 4 (over x, core).
Axes of the slice: x: 2, y: 2, z: 4, core: 2. Of those that a mesh axis runs over, the one named last changes fastest.
Arguments:
- hidden: bfloat16 [1024, 28672], P(('group', 'job'), 'tensor'), parts along dimension 0, may hold values from -6 to 6
- frozen_down_weight: bfloat16 [28672, 8192], P('tensor', 'job'), may hold values from -0.03125 to 0.03125
- adapter_down_matrices: bfloat16 [16, 28672, 64], P(('group', 'job'), 'tensor'), parts along dimension 0, may hold values from -0.03125 to 0.03125
- adapter_up_matrices: bfloat16 [16, 64, 8192], P(('group', 'tensor'), None, 'job'), parts along dimension 0, may hold values from -0.75 to 0.75
- row_block_job_ids: int32 [8], P('group'), parts along dimension 0, may hold values from 0 to 7
- home: int32 [16], P('group'), parts along dimension 0, may hold values from 0 to 7, each once
- cotangent: bfloat16 [1024, 8192], P(('group', 'tensor'), 'job'), parts along dimension 0, may hold values from -6 to 6
Outputs:
- mixed: bfloat16 [1024, 8192], P(('group', 'tensor'), 'job'), parts along dimension 0
- hidden_gradient: bfloat16 [1024, 28672], P(('group', 'job'), 'tensor'), parts along dimension 0
- grad_down: bfloat16 [16, 28672, 64], P(('group', 'job'), 'tensor'), parts along dimension 0
- up_matrix_gradient: bfloat16 [16, 64, 8192], P(('group', 'tensor'), None, 'job'), parts along dimension 0
There are 2 independent parts, one for each index of `group`. A program takes and returns all parts, laid end to end along the dimension named above; an argument that names none is the same for every part. Nothing has to cross between parts.
Inputs may be any that keep to these rules, and one draw needn't show every extreme that they name: `home`: each job names a different storage row; row s of adapter_down_matrices and grad_down lies on the job index that holds row s in their placement, row s of adapter_up_matrices and up_matrix_gradient on the tensor index that holds it in theirs.
All inputs are finite; a program needn't handle non-finite values.
Results may differ from a plain program's by a relative error of at most 0.014.
Values may be sent and summed in bfloat16 or wider, within the bound.
A program may use at most 192 MiB of HBM per device.

v0:
```python
import jax
import jax.numpy as jnp
from jax import lax
from jax.sharding import PartitionSpec as P

BLOCK = 128


adapter_scale = 2.0


def per_device(
    hidden,
    frozen_down_weight,
    adapter_down_matrices,
    adapter_up_matrices,
    row_block_job_ids,
    home,
    cotangent,
):
    row_shard_index, hidden_shard_width = hidden.shape
    shard_row_count, column_shard_index = cotangent.shape
    tensor_count = lax.axis_size("tensor")
    job_count = lax.axis_size("job")
    tensor_pos = lax.axis_index("tensor")
    job_pos = lax.axis_index("job")
    block_total = row_block_job_ids.shape[0]
    local_blocks = row_shard_index // BLOCK
    adapter_rank_width = adapter_down_matrices.shape[2]
    down_matrix_positions = adapter_down_matrices.shape[0]
    up_matrix_positions = adapter_up_matrices.shape[0]
    storage_layout = jnp.take(home, row_block_job_ids)
    down_owner = storage_layout // down_matrix_positions
    down_matrix_position = storage_layout % down_matrix_positions
    up_owner = storage_layout // up_matrix_positions
    up_matrix_position = storage_layout % up_matrix_positions
    slab_blocks = max(shard_row_count // BLOCK, 1)
    slab_sub = min(shard_row_count, BLOCK)
    narrow_zeros = jnp.zeros((), jnp.bfloat16)
    local_ids = jnp.arange(local_blocks, dtype=jnp.int32)
    job_ids = jnp.arange(job_count, dtype=jnp.int32)
    needed_positions = job_ids[:, None] * local_blocks + local_ids[None, :]
    mine_down_matrices = (jnp.take(down_owner, needed_positions) == job_pos)[:, :, None, None]
    send_down = jnp.where(
        mine_down_matrices,
        jnp.take(adapter_down_matrices, jnp.take(down_matrix_position, needed_positions), axis=0),
        narrow_zeros,
    )
    got_down = lax.all_to_all(send_down, "job", split_axis=0, concat_axis=0, tiled=True)
    my_blocks = job_pos * local_blocks + local_ids
    row_block_down_matrix = got_down[jnp.take(down_owner, my_blocks), local_ids]
    hidden_all = lax.all_gather(hidden, "job", axis=0, tiled=True)
    rows = hidden_all
    frozen_weight_shard = lax.psum_scatter(
        jnp.dot(rows, frozen_down_weight, preferred_element_type=jnp.float32).astype(jnp.bfloat16),
        "tensor",
        scatter_dimension=0,
        tiled=True,
    ).astype(jnp.float32)
    inner_part = jnp.einsum(
        "nbf,nfr->nbr",
        hidden.reshape(local_blocks, BLOCK, hidden_shard_width),
        row_block_down_matrix,
        preferred_element_type=jnp.float32,
    )
    inner_sum = lax.psum(inner_part.astype(jnp.bfloat16), "tensor")
    inner_low = inner_sum.reshape(row_shard_index, adapter_rank_width)
    inner_all = lax.all_gather(inner_low, "job", axis=0, tiled=True)
    first_block = tensor_pos * shard_row_count // BLOCK
    slab_range = jnp.arange(slab_blocks, dtype=jnp.int32)
    peer_ids = jnp.arange(tensor_count, dtype=jnp.int32)
    neighbor_row_blocks = peer_ids[:, None] * shard_row_count // BLOCK + slab_range[None, :]
    mine_up_matrices = (jnp.take(up_owner, neighbor_row_blocks) == tensor_pos)[:, :, None, None]
    send_up = jnp.where(
        mine_up_matrices,
        jnp.take(adapter_up_matrices, jnp.take(up_matrix_position, neighbor_row_blocks), axis=0),
        narrow_zeros,
    )
    got_up = lax.all_to_all(send_up, "tensor", split_axis=0, concat_axis=0, tiled=True)
    slab_up = got_up[jnp.take(up_owner, first_block + slab_range), slab_range]
    inner_slab = lax.dynamic_slice_in_dim(
        inner_all, tensor_pos * shard_row_count, shard_row_count, 0
    ).reshape(slab_blocks, slab_sub, adapter_rank_width)
    adapter_output = adapter_scale * jnp.einsum(
        "xzh,xhk->xzk", inner_slab, slab_up, preferred_element_type=jnp.float32
    )
    mixed = (
        frozen_weight_shard + adapter_output.reshape(shard_row_count, column_shard_index)
    ).astype(jnp.bfloat16)
    back_part = jnp.einsum(
        "cgx,csx->cgs",
        cotangent.reshape(slab_blocks, slab_sub, column_shard_index),
        slab_up,
        preferred_element_type=jnp.float32,
    )
    backward_total = lax.psum(back_part, "job")
    backward_narrow = (
        (adapter_scale * backward_total)
        .astype(jnp.bfloat16)
        .reshape(shard_row_count, adapter_rank_width)
    )
    back_all = lax.all_gather(backward_narrow, "tensor", axis=0, tiled=True)
    cot_all = lax.all_gather(cotangent, "tensor", axis=0, tiled=True)
    rows = cot_all
    frozen_backward = lax.psum_scatter(
        lax.dot_general(
            rows, frozen_down_weight, (((1,), (1,)), ((), ())), preferred_element_type=jnp.float32
        ).astype(jnp.bfloat16),
        "job",
        scatter_dimension=0,
        tiled=True,
    ).astype(jnp.float32)
    back_local = lax.dynamic_slice_in_dim(
        back_all, job_pos * row_shard_index, row_shard_index, 0
    ).reshape(local_blocks, BLOCK, adapter_rank_width)
    adapter_backward = jnp.einsum(
        "cet,cqt->ceq", back_local, row_block_down_matrix, preferred_element_type=jnp.float32
    )
    hidden_gradient = (
        frozen_backward + adapter_backward.reshape(row_shard_index, hidden_shard_width)
    ).astype(jnp.bfloat16)
    up_gradient_terms = jnp.einsum(
        "nbr,nbd->nrd",
        inner_all.reshape(block_total, BLOCK, adapter_rank_width),
        cot_all.reshape(block_total, BLOCK, column_shard_index),
        preferred_element_type=jnp.float32,
    )
    up_matrix_arrival = (
        (up_owner == tensor_pos)[:, None]
        & (up_matrix_position[:, None] == jnp.arange(up_matrix_positions, dtype=jnp.int32)[None, :])
    ).astype(jnp.float32)
    up_matrix_gradient = (
        adapter_scale
        * jnp.einsum(
            "xc,xti->cti", up_matrix_arrival, up_gradient_terms, precision=lax.Precision.HIGHEST
        )
    ).astype(jnp.bfloat16)
    down_terms = jnp.einsum(
        "nbf,nbr->nfr",
        hidden_all.reshape(block_total, BLOCK, hidden_shard_width),
        back_all.reshape(block_total, BLOCK, adapter_rank_width),
        preferred_element_type=jnp.float32,
    )
    down_land = (
        (down_owner == job_pos)[:, None]
        & (
            down_matrix_position[:, None]
            == jnp.arange(down_matrix_positions, dtype=jnp.int32)[None, :]
        )
    ).astype(jnp.float32)
    grad_down = jnp.einsum(
        "ns,nfr->sfr", down_land, down_terms, precision=lax.Precision.HIGHEST
    ).astype(jnp.bfloat16)
    return (mixed, hidden_gradient, grad_down, up_matrix_gradient)


def solution(mesh):
    in_specs = (
        P(("group", "job"), "tensor"),
        P("tensor", "job"),
        P(("group", "job"), "tensor", None),
        P(("group", "tensor"), None, "job"),
        P("group"),
        P("group"),
        P(("group", "tensor"), "job"),
    )
    out_specs = (
        P(("group", "tensor"), "job"),
        P(("group", "job"), "tensor"),
        P(("group", "job"), "tensor", None),
        P(("group", "tensor"), None, "job"),
    )
    return jax.shard_map(
        per_device, mesh=mesh, in_specs=in_specs, out_specs=out_specs, check_vma=False
    )
```

profile of v0, /device:TPU:25, one launch (start us, length us, event | category | flops | bytes accessed | tf_op | source)
XLA Modules:
  0.0 333.1 jit_solution(4339018815941250519)
XLA Ops:
  7.2 0.0 copy-start
  7.2 0.0 all-gather.4.cloned.1.call-start
  7.2 0.7 all-gather.4.cloned.1.call-update
  7.9 0.0 all-gather.6.cloned.1.call-start
  8.0 0.7 all-gather.6.cloned.1.call-update
  8.7 0.0 reduce-scatter.3.cloned.1.call-start
  8.7 54.6 %all-gather.4.cloned.1.call-done = bf16[512,7168]{1,0:T(8,128)(2,1)} async-done(((bf16[128,7168]{1,0:T(8,128)(2,1)}), bf16[512,7168]{1,0:T(8,128)(2,1)}) %all-gather.4.cloned.1.call-update) | async-done | bytes 7340048 | tf_op jit(solution)/shard_map/all_gather | solution.py:52
  63.3 23.7 %convolution_convert_fusion.2 = bf16[512,2048]{1,0:T(8,128)(2,1)} fusion(bf16[512,7168]{1,0:T(8,128)(2,1)} %all-gather.4.cloned.1.call-done, bf16[7168,2048]{1,0:T(8,128)(2,1)} %param.10), kind=kOutput, calls=%fused_computation.15 | convolution fusion | flops 15033434112 | bytes 38797312 | tf_op jit(solution)/shard_map/dot_general | solution.py:55
  87.1 0.0 reduce-scatter.3.cloned.1.call-update
  87.1 0.0 reduce-scatter.5.cloned.1.call-start
  87.2 21.3 %all-gather.6.cloned.1.call-done = bf16[512,2048]{1,0:T(8,128)(2,1)} async-done(((bf16[128,2048]{1,0:T(8,128)(2,1)}), bf16[512,2048]{1,0:T(8,128)(2,1)}) %all-gather.6.cloned.1.call-update) | async-done | bytes 2097168 | tf_op jit(solution)/shard_map/all_gather | solution.py:103
  108.5 22.8 %convolution_convert_fusion = bf16[512,7168]{1,0:T(8,128)(2,1)} fusion(bf16[512,2048]{1,0:T(8,128)(2,1)} %all-gather.6.cloned.1.call-done, bf16[7168,2048]{1,0:T(8,128)(2,1)} %param.10), kind=kOutput, calls=%fused_computation.7 | convolution fusion | flops 15036055552 | bytes 38797312 | tf_op jit(solution)/shard_map/dot_general | solution.py:106
  131.3 0.0 copy-start.4
  131.3 0.0 copy-start.1
  131.3 0.0 reduce-scatter.5.cloned.1.call-update
  131.3 0.6 copy-done.4
  132.0 0.0 copy-done.1
  132.0 0.6 gather_fusion
  132.7 0.6 gather_fusion.6
  133.3 0.6 gather_fusion.5
  134.0 0.0 copy-done.2
  134.0 0.6 gather_fusion.2
  134.6 1.2 fusion.8
  135.8 5.7 %all-to-all-start.1 = ((bf16[4,1,64,2048]{3,2,1,0:T(8,128)(2,1)}), bf16[4,1,64,2048]{3,2,1,0:T(8,128)(2,1)S(1)}, u32[]{:S(2)}, u32[]{:S(2)}) async-start(bf16[4,1,64,2048]{3,2,1,0:T(8,128)(2,1)} %fusion.8), calls=%async_computation.2 | async-start | bytes 2097152 | tf_op jit(solution)/shard_map/all_to_all | solution.py:79
  141.5 0.6 gather_fusion.4
  142.1 0.6 gather_fusion.3
  142.8 0.0 copy-done
  142.8 2.6 gather_fusion.1
  145.4 4.4 %fusion.2 = bf16[4,1,7168,64]{2,3,1,0:T(8,128)(2,1)} fusion(bf16[4,7168,64]{1,2,0:T(8,128)(2,1)} %gather_fusion.1, pred[4]{0:T(512)(128)(4,1)S(1)} %get-tuple-element.68, pred[4]{0:T(512)(128)(4,1)S(1)} %get-tuple-element.69), kind=kLoop, calls=%fused_computation.14 | loop fusion | flops 3670016 | bytes 7340040 | tf_op jit(solution)/shard_map/jit(_where)/select_n | solution.py:44
  149.8 25.1 %all-to-all-done.1 = bf16[4,1,64,2048]{3,2,1,0:T(8,128)(2,1)S(1)} async-done(((bf16[4,1,64,2048]{3,2,1,0:T(8,128)(2,1)}), bf16[4,1,64,2048]{3,2,1,0:T(8,128)(2,1)S(1)}, u32[]{:S(2)}, u32[]{:S(2)}) %all-to-all-start.1) | async-done | bytes 1048608 | tf_op jit(solution)/shard_map/all_to_all | solution.py:79
  174.9 5.4 %all-to-all-start = ((bf16[4,1,7168,64]{2,3,1,0:T(8,128)(2,1)}), bf16[4,1,7168,64]{2,3,1,0:T(8,128)(2,1)}, u32[]{:S(2)}, u32[]{:S(2)}) async-start(bf16[4,1,7168,64]{2,3,1,0:T(8,128)(2,1)} %fusion.2), calls=%async_computation.1 | async-start | bytes 7340032 | tf_op jit(solution)/shard_map/all_to_all | solution.py:49
  180.3 0.7 fusion.39
  182.3 0.0 copy-done.3
  182.3 0.3 convolution_bitcast_fusion.1
  182.6 78.0 %psum.15 = f32[1,128,64]{1,2,0:T(8,128)S(1)} all-reduce(f32[1,128,64]{1,2,0:T(8,128)S(1)} %convolution_bitcast_fusion.1), channel_id=1, replica_groups=mesh['group'=2,'tensor'=4,'job'=4] {'job'}, use_global_device_ids=true, to_apply=%region_3.5 | all-reduce | flops 8192 | bytes 65536 | tf_op jit(solution)/shard_map/psum | solution.py:96
  260.6 9.9 %all-gather = bf16[1,512,64]{1,2,0:T(8,128)(2,1)S(1)} all-gather(bf16[1,128,64]{1,2,0:T(8,128)(2,1)S(1)} %multiply_convert_fusion), channel_id=2, replica_groups=mesh['group'=2,'tensor'=4,'job'=4] {'tensor'}, dimensions={1}, use_global_device_ids=true | all-gather | bytes 81920 | tf_op jit(solution)/shard_map/all_gather | solution.py:102
  270.6 0.0 all-to-all-done
  270.6 2.5 fusion.7
  273.1 12.7 %psum.14 = bf16[128,64]{0,1:T(8,128)(2,1)S(1)} all-reduce(bf16[128,64]{0,1:T(8,128)(2,1)S(1)} %fusion.7), channel_id=1, replica_groups=mesh['group'=2,'tensor'=4,'job'=4] {'tensor'}, use_global_device_ids=true, to_apply=%region_1.3 | all-reduce | flops 8192 | bytes 32768 | tf_op jit(solution)/shard_map/psum | solution.py:66
  285.8 11.5 %all_gather.13 = bf16[512,64]{0,1:T(8,128)(2,1)S(1)} all-gather(bf16[128,64]{0,1:T(8,128)(2,1)S(1)} %psum.14), channel_id=1, replica_groups=mesh['group'=2,'tensor'=4,'job'=4] {'job'}, dimensions={0}, use_global_device_ids=true | all-gather | bytes 81920 | tf_op jit(solution)/shard_map/all_gather | solution.py:68
  297.3 2.0 fusion.17
  299.3 3.5 %fusion.4 = bf16[2,64,2048]{2,0,1:T(2,128)(2,1)S(1)} fusion(f32[4,64,2048]{2,1,0:T(8,128)S(1)} %fusion.17, pred[4]{0:T(512)(128)(4,1)S(1)} %get-tuple-element.61, s32[4]{0:T(128)S(1)} %and_select_fusion.1), kind=kOutput, calls=%fused_computation.19 | convolution fusion | flops 13107216 | bytes 2621460 | tf_op jit(solution)/shard_map/xc,xti->cti/dot_general | solution.py:134
  302.8 1.0 copy.20
  303.7 4.2 %convolution_bitcast_fusion = f32[4,7168,64]{1,2,0:T(8,128)S(1)} fusion(bf16[4,128,7168]{2,1,0:T(8,128)(2,1)} %bitcast.95, bf16[4,128,64]{1,0,2:T(4,128)(2,1)S(1)} %reshape.234), kind=kOutput, calls=%fused_computation.8 | convolution fusion | flops 469762048 | bytes 14745600 | tf_op jit(solution)/shard_map/nbf,nbr->nfr/dot_general | solution.py:138
  307.9 11.2 %convolution_convert_fusion.1 = bf16[2,7168,64]{1,0,2:T(2,128)(2,1)S(1)} fusion(f32[4,7168,64]{1,2,0:T(8,128)S(1)} %convolution_bitcast_fusion, pred[4]{0:T(512)(128)(4,1)S(1)} %broadcast_compare_fusion.1, s32[4]{0:T(128)S(1)} %and_select_fusion.1), kind=kOutput, calls=%fused_computation.11 | convolution fusion | flops 44957712 | bytes 9175060 | tf_op jit(solution)/shard_map/ns,nfr->sfr/dot_general | solution.py:151
  319.2 1.6 copy.19
  320.7 2.2 fusion.5
  322.9 3.7 %fusion = bf16[128,7168]{1,0:T(8,128)(2,1)} fusion(bf16[128,7168]{1,0:T(8,128)(2,1)} %reduce-scatter.5.cloned.1.call-done, bf16[4,1,7168,64]{2,3,1,0:T(8,128)(2,1)} %all-to-all-done, s32[]{:T(128)} %bitcast.8, bf16[1,512,64]{1,2,0:T(8,128)(2,1)S(1)} %all-gather, s32[]{:T(128)S(6)} %select_n.161), kind=kOutput, calls=%fused_computation.10 | convolution fusion | flops 120193024 | bytes 4604420 | tf_op jit(solution)/shard_map/cet,cqt->ceq/dot_general | solution.py:116
  (21 shorter events, 0.2 us)
Async XLA Ops:
  7.2 135.6 %copy-start = (bf16[2,7168,64]{1,2,0:T(8,128)(2,1)S(1)}, bf16[2,7168,64]{1,2,0:T(8,128)(2,1)}, u32[]{:S(2)}) copy-start(bf16[2,7168,64]{1,2,0:T(8,128)(2,1)} %param.11) | copy-start | bytes 5505028
  7.2 56.2 %all-gather.4.cloned.1.call-start = ((), (), s32[]{:S(2)}) async-start(), calls=%async_computation.4 | async-start | bytes 9175040 | tf_op jit(solution)/shard_map/all_gather | solution.py:52
  7.9 100.6 %all-gather.6.cloned.1.call-start = ((), (), s32[]{:S(2)}) async-start(), calls=%async_computation.6 | async-start | bytes 2621440 | tf_op jit(solution)/shard_map/all_gather | solution.py:103
  8.7 312.1 %reduce-scatter.3.cloned.1.call-start = ((), (), s32[]{:S(2)}) async-start(), calls=%async_computation.5 | async-start | bytes 2621440 | tf_op jit(solution)/shard_map/reduce_scatter | solution.py:54
  87.1 235.8 %reduce-scatter.5.cloned.1.call-start = ((), (), s32[]{:S(2)}) async-start(), calls=%async_computation.7 | async-start | bytes 9175040 | tf_op jit(solution)/shard_map/reduce_scatter | solution.py:105
  131.3 0.7 copy-start.4
  131.3 0.7 copy-start.1
  131.3 2.7 copy-start.2
  135.8 39.1 %all-to-all-start.1 = ((bf16[4,1,64,2048]{3,2,1,0:T(8,128)(2,1)}), bf16[4,1,64,2048]{3,2,1,0:T(8,128)(2,1)S(1)}, u32[]{:S(2)}, u32[]{:S(2)}) async-start(bf16[4,1,64,2048]{3,2,1,0:T(8,128)(2,1)} %fusion.8), calls=%async_computation.2 | async-start | bytes 2097152 | tf_op jit(solution)/shard_map/all_to_all | solution.py:79
  149.8 32.5 %copy-start.3 = (bf16[128,2048]{1,0:T(8,128)(2,1)S(1)}, bf16[128,2048]{1,0:T(8,128)(2,1)}, u32[]{:S(2)}) copy-start(bf16[128,2048]{1,0:T(8,128)(2,1)} %param.15) | copy-start | bytes 1572868
  174.9 95.7 %all-to-all-start = ((bf16[4,1,7168,64]{2,3,1,0:T(8,128)(2,1)}), bf16[4,1,7168,64]{2,3,1,0:T(8,128)(2,1)}, u32[]{:S(2)}, u32[]{:S(2)}) async-start(bf16[4,1,7168,64]{2,3,1,0:T(8,128)(2,1)} %fusion.2), calls=%async_computation.1 | async-start | bytes 7340032 | tf_op jit(solution)/shard_map/all_to_all | solution.py:49
Sparse Core Ops, SparseCore 0:
  9.6 53.7 all-gather.3
  64.9 43.5 all-gather.5
  110.8 51.9 reduce-scatter.2
  165.4 98.6 reduce-scatter.4
where the time goes:
time: 337 us; the launch traced here: 333 us
  blocking collectives  112 us (33%)
  waiting for transfers between devices  103 us (31%)
  matrix products  76.1 us (23%)
  between operations  15.2 us (5%)
  starting transfers between devices  11.2 us (3%)
  local copies, waits for them, and re-layouts  10.2 us (3%)
  other arithmetic  5.66 us (2%)
    psum x1, blocking collectives, per_device(): backward_total = lax.psum(back_part, 'job')  78 us
    all_gather x1, waiting for transfers between devices, per_device(): hidden_all = lax.all_gather(hidden, 'job', axis=0, tiled=True)  54.6 us
    all_to_all x1, waiting for transfers between devices, per_device(): lax.all_to_all(send_up, 'tensor', split_axis=0, concat_axis=0, tiled=True)  25.1 us
    dot_general x1, matrix products, per_device(): jnp.dot(rows, frozen_down_weight, preferred_element_type=jnp.float32)  23.7 us
    dot_general x1, matrix products, per_device(): lax.dot_general(rows, frozen_down_weight, (((1,), (1,)), ((), ())), prefe...  22.8 us
    all_gather x1, waiting for transfers between devices, per_device(): cot_all = lax.all_gather(cotangent, 'tensor', axis=0, tiled=True)  21.3 us
    psum x1, blocking collectives, per_device(): inner_sum = lax.psum(inner_part.astype(jnp.bfloat16), 'tensor')  12.7 us
    all_gather x1, blocking collectives, per_device(): inner_all = lax.all_gather(inner_low, 'job', axis=0, tiled=True)  11.5 us
  transfers between devices with their start and end apart: 6, of which 3 were waited for; matrix products, arithmetic and copies ran while one was open for 26% of the time, Pallas kernels for 0%

commit v1 on v0

v1 whole, which is shorter than its diff:
```python
import functools

import jax
import jax.numpy as jnp
from jax import lax
from jax.experimental import pallas as pl
from jax.experimental.pallas import tpu as pltpu
from jax.sharding import PartitionSpec as P

BLOCK = 128
RANK = 64
adapter_scale = 2.0
MESH = pl.DeviceIdType.MESH
F32 = jnp.float32
BF16 = jnp.bfloat16
NT = (((1,), (1,)), ((), ()))
TN = (((0,), (0,)), ((), ()))


def nn_dot(a, b):
    return jnp.dot(a, b, preferred_element_type=F32)


def nt_dot(a, b):
    return lax.dot_general(a, b, NT, preferred_element_type=F32)


def tn_dot(a, b):
    return lax.dot_general(a, b, TN, preferred_element_type=F32)


def fold_matrix(height):
    row = lax.broadcasted_iota(jnp.int32, (height, 2 * RANK), 0)
    lane = lax.broadcasted_iota(jnp.int32, (height, 2 * RANK), 1)
    return jnp.where(row % RANK == lane % RANK, 1.0, 0.0).astype(BF16)


def spread_matrix(first):
    row = lax.broadcasted_iota(jnp.int32, (2 * RANK, 2 * RANK), 0)
    lane = lax.broadcasted_iota(jnp.int32, (2 * RANK, 2 * RANK), 1)
    return jnp.where(row == lane % RANK + first, 1.0, 0.0).astype(BF16)


def step_kernel(
    T, J, ft, ct, chunks,
    hid, w, dn, up, mdn, mup, cot,
    mixed, hg, gd, ug,
    wv, hall, call, dnv, bpb, prv, xrv, fa, mst, mrv, ugv,
    backcat, innercat, pack, brt, brj, irt, irj,
    loc, c_s, c_r, hp_s, hp_r, ho_s, ho_r, hf_s, hf_r,
    b1_s, b1_r, b2_s, b2_r, i1_s, i1_r, i2_s, i2_r,
    ps, pr, xs, xr, ms, mr, outs,
):
    j = lax.axis_index("job")
    t = lax.axis_index("tensor")
    F, C = w.shape
    hr = hid.shape[0]
    cr = cot.shape[0]
    R = hr * J
    NP = J // 2
    nd = dn.shape[1] // RANK
    nu = up.shape[0] // RANK
    px = j // 2
    c = j % 2
    partner = 2 * px + 1 - c
    half = R // 2
    nft = F // ft
    nct = C // ct
    fch = F // chunks

    def remote(src, dst, s, r, axis, index):
        return pltpu.make_async_remote_copy(
            src_ref=src, dst_ref=dst, send_sem=s, recv_sem=r,
            device_id={axis: index}, device_id_type=MESH,
        )

    load_w = pltpu.make_async_copy(w, wv, loc.at[0])
    load_h = pltpu.make_async_copy(hid, hall.at[j], loc.at[1])
    load_c = pltpu.make_async_copy(cot, call.at[t], loc.at[2])
    load_d = pltpu.make_async_copy(dn, dnv, loc.at[3])
    load_h.start()
    load_w.start()
    load_c.start()
    load_d.start()

    barrier = pltpu.get_barrier_semaphore()
    for d in range(1, J):
        pl.semaphore_signal(barrier, inc=1, device_id={"job": (j + d) % J}, device_id_type=MESH)
    for d in range(1, T):
        pl.semaphore_signal(barrier, inc=1, device_id={"tensor": (t + d) % T}, device_id_type=MESH)
    pl.semaphore_wait(barrier, J + T - 2)

    sent = []
    outer = {}
    for ch in range(chunks):
        cols = pl.ds(ch * fch, fch)
        for d in range(1, NP):
            copy = remote(
                hid.at[:, cols], hall.at[j, :, cols],
                ho_s.at[d - 1, ch], ho_r.at[d - 1, ch], "job", (j + 2 * d) % J,
            )
            copy.start()
            outer[d, ch] = copy
            sent.append(copy)
    to_partner = remote(hid, hall.at[j], hp_s.at[0], hp_r.at[0], "job", partner)
    to_partner.start()
    sent.append(to_partner)
    cot_copies = []
    for d in range(1, T):
        copy = remote(cot, call.at[t], c_s.at[d - 1], c_r.at[d - 1], "tensor", (t + d) % T)
        copy.start()
        cot_copies.append(copy)
        sent.append(copy)

    load_h.wait()
    load_w.wait()
    to_partner.wait_recv()

    def columns(n):
        return pl.ds(pl.multiple_of(n * ct, ct), ct)

    @pl.loop(0, nct)
    def _(n):
        rows = hall[pl.ds(2 * px, 2)].reshape(2 * hr, F)
        fa[:, columns(n)] = nn_dot(rows, wv[:, columns(n)])

    forwards = []
    for ch in range(chunks):
        cols = pl.ds(ch * fch, fch)
        for d in range(1, NP):
            outer[d, ch].wait_recv()
            source = (j - 2 * d + J) % J
            part = hall.at[source, :, cols]
            copy = remote(part, part, hf_s.at[d - 1, ch], hf_r.at[d - 1, ch], "job", partner)
            copy.start()
            forwards.append(copy)
            sent.append(copy)

    lane_low = lax.broadcasted_iota(jnp.int32, (half, 2 * RANK), 1) < RANK

    def packed(masked, height):
        both = nn_dot(masked, fold_matrix(height))
        return jnp.where(lane_low, both[:half], both[half:]).astype(BF16)

    def send_all(src, land, s, r, axis, index, count):
        copies = []
        for d in range(1, count):
            copy = remote(src, land.at[d - 1], s.at[d - 1], r.at[d - 1], axis, (index + d) % count)
            copy.start()
            copies.append(copy)
            sent.append(copy)
        return copies

    def total_of(src, land, copies):
        total = src[...].astype(F32)
        for d, copy in enumerate(copies):
            copy.wait_recv()
            total = total + land[d].astype(F32)
        return total

    def spread(short, width):
        both = jnp.concatenate(
            [nn_dot(short, spread_matrix(0)), nn_dot(short, spread_matrix(RANK))], axis=0
        )
        return jnp.concatenate([both] * (width // 2), axis=1)

    load_c.wait()
    for copy in cot_copies:
        copy.wait_recv()
    part = nt_dot(call[...].reshape(R, C), up[...])
    pack[0] = packed((part * mup[...].astype(F32)).astype(BF16), nu * RANK)
    back_one = send_all(pack.at[0], brt, b1_s, b1_r, "tensor", t, T)

    load_d.wait()
    for copy in forwards:
        copy.wait_recv()

    @pl.loop(0, J)
    def _(b):
        rows = pl.ds(pl.multiple_of(b * hr, hr), hr)
        value = nn_dot(hall[b], dnv[...])
        backcat[rows] = (value * mdn[rows].astype(F32)).astype(BF16)

    pack[1] = packed(backcat[...], nd * RANK)
    inner_one = send_all(pack.at[1], irj, i1_s, i1_r, "job", j, J)
    pack[2] = total_of(pack.at[0], brt, back_one).astype(BF16)
    back_two = send_all(pack.at[2], brj, b2_s, b2_r, "job", j, J)
    pack[3] = total_of(pack.at[1], irj, inner_one).astype(BF16)
    inner_two = send_all(pack.at[3], irt, i2_s, i2_r, "tensor", t, T)
    back = (adapter_scale * total_of(pack.at[2], brj, back_two)).astype(BF16)
    backcat[...] = (spread(back, nd) * mdn[...].astype(F32)).astype(BF16)
    inner = total_of(pack.at[3], irt, inner_two).astype(BF16)
    innercat[...] = (adapter_scale * spread(inner, nu) * mup[...].astype(F32)).astype(BF16)

    blocks = 2 * hr // cr

    def mixed_copy(d):
        to = (t + d) % T
        return to, remote(mst.at[to], mrv.at[d - 1], ms.at[d - 1], mr.at[d - 1], "tensor", to)

    def pair_rows(pair):
        return pl.ds(pl.multiple_of(pair * 2 * hr, 2 * hr), 2 * hr)

    @pl.loop(0, nct)
    def _(n):
        value = fa[:, columns(n)] + nn_dot(innercat[pair_rows(px)], up[:, columns(n)])
        mst[pl.ds(px * blocks, blocks), :, columns(n)] = value.astype(BF16).reshape(blocks, cr, ct)

    for d in range(1, T):
        to, copy = mixed_copy(d)

        @pl.when(to // blocks == px)
        def _():
            copy.start()

    def tile(k):
        return pl.ds(pl.multiple_of(k * ft, ft), ft)

    def pair_copy(k):
        return remote(
            bpb.at[:, 1 - c, :, tile(k)], prv.at[:, :, tile(k)], ps.at[k], pr.at[k], "job", partner
        )

    def outer_copy(d, k):
        to = (j + 2 * d) % J
        return remote(
            bpb.at[to // 2, c, :, tile(k)], xrv.at[d - 1, :, tile(k)],
            xs.at[d - 1, k], xr.at[d - 1, k], "job", to,
        )

    def pass_on(k):
        pair_copy(k).wait_recv()
        both = bpb[:, c, :, tile(k)].astype(F32) + prv[:, :, tile(k)].astype(F32)
        bpb[:, c, :, tile(k)] = both.astype(BF16)
        for d in range(1, NP):
            outer_copy(d, k).start()

    @pl.loop(0, nft)
    def _(k):
        value = nt_dot(call[...].reshape(R, C), wv[tile(k)])
        value = value + nt_dot(backcat[...], dnv[tile(k)])
        bpb[:, :, :, tile(k)] = value.astype(BF16).reshape(NP, 2, hr, ft)
        pair_copy(k).start()
        grad = tn_dot(hall[:, :, tile(k)].reshape(R, ft), backcat[...])
        dnv[tile(k)] = grad.astype(BF16)

        @pl.when(k > 0)
        def _():
            pass_on(k - 1)

    pass_on(nft - 1)
    out_gd = pltpu.make_async_copy(dnv, gd, outs.at[0])
    out_gd.start()

    for e in range(1, NP):
        pair = (px + e) % NP

        @pl.loop(0, nct)
        def _(n):
            rows = hall[pl.ds(2 * pair, 2)].reshape(2 * hr, F)
            value = nn_dot(rows, wv[:, columns(n)])
            value = value + nn_dot(innercat[pair_rows(pair)], up[:, columns(n)])
            mst[pl.ds(pair * blocks, blocks), :, columns(n)] = value.astype(BF16).reshape(
                blocks, cr, ct
            )

        for d in range(1, T):
            to, copy = mixed_copy(d)

            @pl.when(to // blocks == pair)
            def _():
                copy.start()

    @pl.loop(0, nct)
    def _(n):
        cots = call[:, :, columns(n)].reshape(R, ct)
        ugv[:, columns(n)] = tn_dot(innercat[...], cots).astype(BF16)

    out_ug = pltpu.make_async_copy(ugv, ug, outs.at[1])
    out_ug.start()

    @pl.loop(0, nft)
    def _(k):
        value = bpb[px, c, :, tile(k)].astype(F32)
        for d in range(1, NP):
            outer_copy(d, k).wait_recv()
            value = value + xrv[d - 1, :, tile(k)].astype(F32)
        bpb[px, c, :, tile(k)] = value.astype(BF16)

    out_hg = pltpu.make_async_copy(bpb.at[px, c], hg, outs.at[2])
    out_hg.start()

    for d in range(1, T):
        mixed_copy(d)[1].wait_recv()

    @pl.loop(0, nct)
    def _(n):
        value = mst[t, :, columns(n)].astype(F32)
        for d in range(1, T):
            value = value + mrv[d - 1, :, columns(n)].astype(F32)
        mst[t, :, columns(n)] = value.astype(BF16)

    out_mx = pltpu.make_async_copy(mst.at[t], mixed, outs.at[3])
    out_mx.start()

    for copy in sent:
        copy.wait_send()
    for d in range(1, T):
        mixed_copy(d)[1].wait_send()

    @pl.loop(0, nft)
    def _(k):
        pair_copy(k).wait_send()
        for d in range(1, NP):
            outer_copy(d, k).wait_send()

    out_gd.wait()
    out_ug.wait()
    out_hg.wait()
    out_mx.wait()


def per_device(hidden, weight, downs, ups, block_jobs, home, cotangent):
    hr, F = hidden.shape
    cr, C = cotangent.shape
    T = lax.axis_size("tensor")
    J = lax.axis_size("job")
    R = hr * J
    NP = J // 2
    nd, nu = downs.shape[0], ups.shape[0]
    storage = jnp.repeat(jnp.take(home, block_jobs), BLOCK)[:, None]
    ndl, nul = nd * RANK, nu * RANK
    own_down = lax.axis_index("job") * nd + jnp.arange(ndl, dtype=jnp.int32)[None, :] // RANK
    own_up = lax.axis_index("tensor") * nu + jnp.arange(nul, dtype=jnp.int32)[None, :] // RANK
    mdn = (storage == own_down).astype(BF16)
    mup = (storage == own_up).astype(BF16)
    dn = jnp.transpose(downs, (1, 0, 2)).reshape(F, ndl)
    up = ups.reshape(nul, C)
    ft = 512 if F % 512 == 0 else 128
    ct = 256
    chunks = 4 if F % 512 == 0 else 1
    nft = F // ft
    sem = pltpu.SemaphoreType.DMA
    anyspace = pl.BlockSpec(memory_space=pl.ANY)
    vmem = pl.BlockSpec(memory_space=pltpu.VMEM)
    n_out = max(NP - 1, 1)
    mixed, hg, gd, ug = pl.pallas_call(
        functools.partial(step_kernel, T, J, ft, ct, chunks),
        out_shape=(
            jax.ShapeDtypeStruct((cr, C), BF16),
            jax.ShapeDtypeStruct((hr, F), BF16),
            jax.ShapeDtypeStruct((F, ndl), BF16),
            jax.ShapeDtypeStruct((nul, C), BF16),
        ),
        in_specs=[anyspace, anyspace, anyspace, vmem, vmem, vmem, anyspace],
        out_specs=(anyspace,) * 4,
        scratch_shapes=[
            pltpu.VMEM((F, C), BF16),
            pltpu.VMEM((J, hr, F), BF16),
            pltpu.VMEM((T, cr, C), BF16),
            pltpu.VMEM((F, ndl), BF16),
            pltpu.VMEM((NP, 2, hr, F), BF16),
            pltpu.VMEM((NP, hr, F), BF16),
            pltpu.VMEM((n_out, hr, F), BF16),
            pltpu.VMEM((2 * hr, C), F32),
            pltpu.VMEM((T, cr, C), BF16),
            pltpu.VMEM((T - 1, cr, C), BF16),
            pltpu.VMEM((nul, C), BF16),
            pltpu.VMEM((R, ndl), BF16),
            pltpu.VMEM((R, nul), BF16),
            pltpu.VMEM((4, R // 2, 2 * RANK), BF16),
            pltpu.VMEM((T - 1, R // 2, 2 * RANK), BF16),
            pltpu.VMEM((J - 1, R // 2, 2 * RANK), BF16),
            pltpu.VMEM((T - 1, R // 2, 2 * RANK), BF16),
            pltpu.VMEM((J - 1, R // 2, 2 * RANK), BF16),
            sem((4,)),
            sem((T - 1,)), sem((T - 1,)),
            sem((1,)), sem((1,)),
            sem((n_out, chunks)), sem((n_out, chunks)),
            sem((n_out, chunks)), sem((n_out, chunks)),
            sem((T - 1,)), sem((T - 1,)), sem((J - 1,)), sem((J - 1,)),
            sem((J - 1,)), sem((J - 1,)), sem((T - 1,)), sem((T - 1,)),
            sem((nft,)), sem((nft,)),
            sem((n_out, nft)), sem((n_out, nft)),
            sem((T - 1,)), sem((T - 1,)),
            sem((4,)),
        ],
        compiler_params=pltpu.CompilerParams(
            collective_id=0, has_side_effects=True, vmem_limit_bytes=64 * 1024 * 1024
        ),
    )(hidden, weight, dn, up, mdn, mup, cotangent)
    grad_down = jnp.transpose(gd.reshape(F, nd, RANK), (1, 0, 2))
    return mixed, hg, grad_down, ug.reshape(nu, RANK, C)


def solution(mesh):
    in_specs = (
        P(("group", "job"), "tensor"),
        P("tensor", "job"),
        P(("group", "job"), "tensor", None),
        P(("group", "tensor"), None, "job"),
        P("group"),
        P("group"),
        P(("group", "tensor"), "job"),
    )
    out_specs = (
        P(("group", "tensor"), "job"),
        P(("group", "job"), "tensor"),
        P(("group", "job"), "tensor", None),
        P(("group", "tensor"), None, "job"),
    )
    return jax.shard_map(
        per_device, mesh=mesh, in_specs=in_specs, out_specs=out_specs, check_vma=False
    )
```

time: 337 us -> 172 us (0.51); the launches traced: 333 us -> 171 us
  Pallas kernels: 0 us -> 156 us
  blocking collectives: 112 us -> 0 us
  waiting for transfers between devices: 103 us -> 0 us
  matrix products: 76.1 us -> 0 us
  between operations: 15.2 us -> 0.67 us
  starting transfers between devices: 11.2 us -> 0 us
  other arithmetic: 5.66 us -> 2.17 us
    pallas_call x0 -> x1, Pallas kernels: none -> 156 us  [per_device(): pl.pallas_call(functools.partial(step_kernel, T, J, ft, ct, chunks), out_...]
    psum x2 -> x0, blocking collectives: 90.7 us -> none  [the longest x1 78 us: per_device(): backward_total = lax.psum(back_part, 'job')]
    dot_general x10 -> x0, matrix products: 76.1 us -> none  [the longest x1 23.7 us: per_device(): jnp.dot(rows, frozen_down_weight, preferred_element_type=jnp.float32)]
    all_gather x2 -> x0, waiting for transfers between devices: 76 us -> none  [the longest x1 54.6 us: per_device(): hidden_all = lax.all_gather(hidden, 'job', axis=0, tiled=True)]
    all_to_all x2 -> x0, waiting for transfers between devices: 25.1 us -> none  [the longest x1 25.1 us: per_device(): lax.all_to_all(send_up, 'tensor', split_axis=0, concat_axis=0, tiled=True)]
    all_gather x2 -> x0, blocking collectives: 21.4 us -> none  [the longest x1 11.5 us: per_device(): inner_all = lax.all_gather(inner_low, 'job', axis=0, tiled=True)]
    all_to_all x2 -> x0, starting transfers between devices: 11.1 us -> none  [the longest x1 5.67 us: per_device(): lax.all_to_all(send_up, 'tensor', split_axis=0, concat_axis=0, tiled=True)]
    gather x8 -> x1, local copies, waits for them, and re-layouts: 7.07 us -> 1.29 us  [per_device(): storage = jnp.repeat(jnp.take(home, block_jobs), BLOCK)[:, None]]
  transfers between devices with their start and end apart: 6 -> 0, of which waited for: 3 -> 0; matrix products, arithmetic and copies ran while one was open for 26% -> 0% of each run, Pallas kernels for 0% -> 0%
where the time goes in v1:
time: 172 us; the launch traced here: 171 us
  Pallas kernels  156 us (91%)
  local copies, waits for them, and re-layouts  12.3 us (7%)
  other arithmetic  2.17 us (1%)
    pallas_call x1, Pallas kernels, per_device(): pl.pallas_call(functools.partial(step_kernel, T, J, ft, ct, chunks), out_...  156 us
    pallas_call x1, local copies, waits for them, and re-layouts, per_device(): pl.pallas_call(functools.partial(step_kernel, T, J, ft, ct, chunks), out_...  4.03 us
    reshape x1, local copies, waits for them, and re-layouts, per_device(): dn = jnp.transpose(downs, (1, 0, 2)).reshape(F, ndl)  3.87 us

profile of v1, /device:TPU:25, one launch (start us, length us, event | category | flops | bytes accessed | tf_op | source)
XLA Modules:
  0.0 171.5 jit_solution(9220627537232314279)
XLA Ops:
  0.6 0.7 compare_select_fusion
  1.3 1.3 gather_fusion
  2.6 0.7 and_select_fusion.1
  3.3 0.1 broadcast_bitcast_fusion
  3.3 0.8 compare_convert_fusion
  4.2 3.9 %copy.13.dn = bf16[7168,128]{1,0:T(8,128)(2,1)} copy(bf16[7168,128]{0,1:T(8,128)(2,1)} %bitcast.10) | data formatting | bytes 3670016 | tf_op jit(solution)/shard_map/reshape | solution.py:337
  8.1 156.4 %shard_map.102 = (bf16[128,2048]{1,0:T(8,128)(2,1)}, bf16[128,7168]{1,0:T(8,128)(2,1)}, bf16[7168,128]{1,0:T(8,128)(2,1)}, bf16[128,2048]{1,0:T(8,128)(2,1)}) custom-call(bf16[128,7168]{1,0:T(8,128)(2,1)} %hid.1, bf16[7168,2048]{1,0:T(8,128)(2,1)} %w.1, bf16[7168,128]{1,0:T(8,128)(2,1)} %copy.13.dn, bf16[128,2048]{1,0:T(8,128)(2,1)} %bitcast.12, ...), custom_call_target="tpu_custom_call" | custom-call | tf_op jit(solution)/shard_map/pallas_call | solution.py:347
  164.4 0.0 copy-start.2
  164.5 0.0 copy-start
  164.5 4.0 %copy.14 = bf16[7168,128]{0,1:T(8,128)(2,1)} copy(bf16[7168,128]{1,0:T(8,128)(2,1)} %get-tuple-element.10) | data formatting | bytes 3670016 | tf_op jit(solution)/shard_map/pallas_call | solution.py:347
  168.5 0.0 copy-done.2
  168.5 0.8 copy.18
  169.3 0.0 copy-done
  169.3 0.0 copy-start.1
  169.3 1.2 copy.19
  170.5 0.2 copy-done.1
  170.7 0.8 copy.20
  (2 shorter events, 0.0 us)
Async XLA Ops:
  164.4 4.1 %copy-start.2 = (bf16[128,2048]{1,0:T(8,128)(2,1)S(1)}, bf16[128,2048]{1,0:T(8,128)(2,1)}, u32[]{:S(2)}) copy-start(bf16[128,2048]{1,0:T(8,128)(2,1)} %get-tuple-element.20) | copy-start | bytes 1572868
  164.5 4.8 %copy-start = (bf16[128,7168]{1,0:T(8,128)(2,1)S(1)}, bf16[128,7168]{1,0:T(8,128)(2,1)}, u32[]{:S(2)}) copy-start(bf16[128,7168]{1,0:T(8,128)(2,1)} %get-tuple-element.21) | copy-start | bytes 5505028
  169.3 1.4 copy-start.1

commit v2 on v1

--- a/solution.py
+++ b/solution.py
@@ -43,10 +43,10 @@
 
 def step_kernel(
     T, J, ft, ct, chunks,
-    hid, w, dn, up, mdn, mup, cot,
+    hid, w, dn, up, ids, home, cot,
     mixed, hg, gd, ug,
     wv, hall, call, dnv, bpb, prv, xrv, fa, mst, mrv, ugv,
-    backcat, innercat, pack, brt, brj, irt, irj,
+    mdn, mup, backcat, innercat, pack, brt, brj, irt, irj,
     loc, c_s, c_r, hp_s, hp_r, ho_s, ho_r, hf_s, hf_r,
     b1_s, b1_r, b2_s, b2_r, i1_s, i1_r, i2_s, i2_r,
     ps, pr, xs, xr, ms, mr, outs,
@@ -58,7 +58,7 @@
     cr = cot.shape[0]
     R = hr * J
     NP = J // 2
-    nd = dn.shape[1] // RANK
+    nd = dn.shape[0] // RANK
     nu = up.shape[0] // RANK
     px = j // 2
     c = j % 2
@@ -82,6 +82,13 @@
     load_w.start()
     load_c.start()
     load_d.start()
+
+    for b in range(R // BLOCK):
+        row = home[ids[b]]
+        rows = slice(b * BLOCK, (b + 1) * BLOCK)
+        for mask, first, count in ((mdn, j * nd, nd), (mup, t * nu, nu)):
+            lane = lax.broadcasted_iota(jnp.int32, (BLOCK, count * RANK), 1)
+            mask[rows] = jnp.where(lane // RANK + first == row, 1.0, 0.0).astype(BF16)
 
     barrier = pltpu.get_barrier_semaphore()
     for d in range(1, J):
@@ -105,27 +112,35 @@
     to_partner = remote(hid, hall.at[j], hp_s.at[0], hp_r.at[0], "job", partner)
     to_partner.start()
     sent.append(to_partner)
-    cot_copies = []
-    for d in range(1, T):
-        copy = remote(cot, call.at[t], c_s.at[d - 1], c_r.at[d - 1], "tensor", (t + d) % T)
-        copy.start()
-        cot_copies.append(copy)
-        sent.append(copy)
-
-    load_h.wait()
-    load_w.wait()
-    to_partner.wait_recv()
-
-    def columns(n):
-        return pl.ds(pl.multiple_of(n * ct, ct), ct)
-
-    @pl.loop(0, nct)
-    def _(n):
-        rows = hall[pl.ds(2 * px, 2)].reshape(2 * hr, F)
-        fa[:, columns(n)] = nn_dot(rows, wv[:, columns(n)])
+
+    def line_copy(step, up_way):
+        block = t - step if up_way else t + step
+        here = jnp.clip(block, 0, T - 1)
+        src = cot if step == 0 else call.at[here]
+        way = 0 if up_way else 1
+        to = (t + 1) % T if up_way else (t + T - 1) % T
+        copy = remote(src, call.at[here], c_s.at[way, step], c_r.at[way, step], "tensor", to)
+        sends = ((block >= 0) & (t + 1 < T)) if up_way else ((block < T) & (t >= 1))
+        lands = (t - 1 - step >= 0) if up_way else (t + 1 + step < T)
+        return copy, sends, lands
+
+    def line_each(step, act, landing):
+        for up_way in (True, False):
+            copy, sends, lands = line_copy(step, up_way)
+
+            @pl.when(lands if landing else sends)
+            def _():
+                act(copy)
+
+    def line_step(step):
+        if step > 0:
+            line_each(step - 1, lambda copy: copy.wait_recv(), True)
+        if step < T - 1:
+            line_each(step, lambda copy: copy.start(), False)
 
     forwards = []
-    for ch in range(chunks):
+
+    def forward(ch):
         cols = pl.ds(ch * fch, fch)
         for d in range(1, NP):
             outer[d, ch].wait_recv()
@@ -136,6 +151,32 @@
             forwards.append(copy)
             sent.append(copy)
 
+    line_step(0)
+
+    load_h.wait()
+    load_w.wait()
+    to_partner.wait_recv()
+
+    def columns(n):
+        return pl.ds(pl.multiple_of(n * ct, ct), ct)
+
+    def own_forward(n):
+        rows = hall[pl.ds(2 * px, 2)].reshape(2 * hr, F)
+        fa[:, columns(n)] = nn_dot(rows, wv[:, columns(n)])
+
+    early = min(2, chunks)
+    forward(0)
+    line_step(1)
+    pl.loop(0, nct // 2)(own_forward)
+    for ch in range(1, early):
+        forward(ch)
+    line_step(2)
+    pl.loop(nct // 2, nct)(own_forward)
+    for ch in range(early, chunks - 1):
+        forward(ch)
+    for step in range(3, T):
+        line_step(step)
+
     lane_low = lax.broadcasted_iota(jnp.int32, (half, 2 * RANK), 1) < RANK
 
     def packed(masked, height):
@@ -165,11 +206,13 @@
         return jnp.concatenate([both] * (width // 2), axis=1)
 
     load_c.wait()
-    for copy in cot_copies:
-        copy.wait_recv()
     part = nt_dot(call[...].reshape(R, C), up[...])
     pack[0] = packed((part * mup[...].astype(F32)).astype(BF16), nu * RANK)
     back_one = send_all(pack.at[0], brt, b1_s, b1_r, "tensor", t, T)
+    if chunks > early:
+        forward(chunks - 1)
+    pack[2] = total_of(pack.at[0], brt, back_one).astype(BF16)
+    back_two = send_all(pack.at[2], brj, b2_s, b2_r, "job", j, J)
 
     load_d.wait()
     for copy in forwards:
@@ -178,19 +221,13 @@
     @pl.loop(0, J)
     def _(b):
         rows = pl.ds(pl.multiple_of(b * hr, hr), hr)
-        value = nn_dot(hall[b], dnv[...])
+        value = nt_dot(hall[b], dnv[...])
         backcat[rows] = (value * mdn[rows].astype(F32)).astype(BF16)
 
     pack[1] = packed(backcat[...], nd * RANK)
     inner_one = send_all(pack.at[1], irj, i1_s, i1_r, "job", j, J)
-    pack[2] = total_of(pack.at[0], brt, back_one).astype(BF16)
-    back_two = send_all(pack.at[2], brj, b2_s, b2_r, "job", j, J)
-    pack[3] = total_of(pack.at[1], irj, inner_one).astype(BF16)
-    inner_two = send_all(pack.at[3], irt, i2_s, i2_r, "tensor", t, T)
     back = (adapter_scale * total_of(pack.at[2], brj, back_two)).astype(BF16)
     backcat[...] = (spread(back, nd) * mdn[...].astype(F32)).astype(BF16)
-    inner = total_of(pack.at[3], irt, inner_two).astype(BF16)
-    innercat[...] = (adapter_scale * spread(inner, nu) * mup[...].astype(F32)).astype(BF16)
 
     blocks = 2 * hr // cr
 
@@ -200,18 +237,6 @@
 
     def pair_rows(pair):
         return pl.ds(pl.multiple_of(pair * 2 * hr, 2 * hr), 2 * hr)
-
-    @pl.loop(0, nct)
-    def _(n):
-        value = fa[:, columns(n)] + nn_dot(innercat[pair_rows(px)], up[:, columns(n)])
-        mst[pl.ds(px * blocks, blocks), :, columns(n)] = value.astype(BF16).reshape(blocks, cr, ct)
-
-    for d in range(1, T):
-        to, copy = mixed_copy(d)
-
-        @pl.when(to // blocks == px)
-        def _():
-            copy.start()
 
     def tile(k):
         return pl.ds(pl.multiple_of(k * ft, ft), ft)
@@ -235,28 +260,21 @@
         for d in range(1, NP):
             outer_copy(d, k).start()
 
-    @pl.loop(0, nft)
-    def _(k):
+    def backward(k):
         value = nt_dot(call[...].reshape(R, C), wv[tile(k)])
-        value = value + nt_dot(backcat[...], dnv[tile(k)])
+        value = value + nn_dot(backcat[...], dnv[:, tile(k)])
         bpb[:, :, :, tile(k)] = value.astype(BF16).reshape(NP, 2, hr, ft)
         pair_copy(k).start()
-        grad = tn_dot(hall[:, :, tile(k)].reshape(R, ft), backcat[...])
-        dnv[tile(k)] = grad.astype(BF16)
+        grad = tn_dot(backcat[...], hall[:, :, tile(k)].reshape(R, ft))
+        dnv[:, tile(k)] = grad.astype(BF16)
 
         @pl.when(k > 0)
         def _():
             pass_on(k - 1)
 
-    pass_on(nft - 1)
-    out_gd = pltpu.make_async_copy(dnv, gd, outs.at[0])
-    out_gd.start()
-
-    for e in range(1, NP):
-        pair = (px + e) % NP
-
-        @pl.loop(0, nct)
-        def _(n):
+    def other_forward(n):
+        for e in range(1, NP):
+            pair = (px + e) % NP
             rows = hall[pl.ds(2 * pair, 2)].reshape(2 * hr, F)
             value = nn_dot(rows, wv[:, columns(n)])
             value = value + nn_dot(innercat[pair_rows(pair)], up[:, columns(n)])
@@ -264,12 +282,49 @@
                 blocks, cr, ct
             )
 
-        for d in range(1, T):
-            to, copy = mixed_copy(d)
-
-            @pl.when(to // blocks == pair)
-            def _():
-                copy.start()
+    first = nft // 7
+    second = 2 * first
+    pl.loop(0, first)(backward)
+    pack[3] = total_of(pack.at[1], irj, inner_one).astype(BF16)
+    inner_two = send_all(pack.at[3], irt, i2_s, i2_r, "tensor", t, T)
+    pl.loop(first, second)(backward)
+    inner = total_of(pack.at[3], irt, inner_two).astype(BF16)
+    innercat[...] = (adapter_scale * spread(inner, nu) * mup[...].astype(F32)).astype(BF16)
+
+    @pl.loop(0, nct)
+    def _(n):
+        value = fa[:, columns(n)] + nn_dot(innercat[pair_rows(px)], up[:, columns(n)])
+        mst[pl.ds(px * blocks, blocks), :, columns(n)] = value.astype(BF16).reshape(blocks, cr, ct)
+
+    for d in range(1, T):
+        to, copy = mixed_copy(d)
+
+        @pl.when(to // blocks == px)
+        def _():
+            copy.start()
+
+    third = second
+    if nct <= nft - second:
+        third = second + nct
+
+        @pl.loop(0, nct)
+        def _(n):
+            other_forward(n)
+            backward(second + n)
+    else:
+        pl.loop(0, nct)(other_forward)
+
+    for d in range(1, T):
+        to, copy = mixed_copy(d)
+
+        @pl.when(to // blocks != px)
+        def _():
+            copy.start()
+
+    pl.loop(third, nft)(backward)
+    pass_on(nft - 1)
+    out_gd = pltpu.make_async_copy(dnv, gd, outs.at[0])
+    out_gd.start()
 
     @pl.loop(0, nct)
     def _(n):
@@ -305,6 +360,8 @@
 
     for copy in sent:
         copy.wait_send()
+    for step in range(T - 1):
+        line_each(step, lambda copy: copy.wait_send(), False)
     for d in range(1, T):
         mixed_copy(d)[1].wait_send()
 
@@ -328,13 +385,8 @@
     R = hr * J
     NP = J // 2
     nd, nu = downs.shape[0], ups.shape[0]
-    storage = jnp.repeat(jnp.take(home, block_jobs), BLOCK)[:, None]
     ndl, nul = nd * RANK, nu * RANK
-    own_down = lax.axis_index("job") * nd + jnp.arange(ndl, dtype=jnp.int32)[None, :] // RANK
-    own_up = lax.axis_index("tensor") * nu + jnp.arange(nul, dtype=jnp.int32)[None, :] // RANK
-    mdn = (storage == own_down).astype(BF16)
-    mup = (storage == own_up).astype(BF16)
-    dn = jnp.transpose(downs, (1, 0, 2)).reshape(F, ndl)
+    dn = jnp.transpose(downs, (0, 2, 1)).reshape(ndl, F)
     up = ups.reshape(nul, C)
     ft = 512 if F % 512 == 0 else 128
     ct = 256
@@ -342,6 +394,7 @@
     nft = F // ft
     sem = pltpu.SemaphoreType.DMA
     anyspace = pl.BlockSpec(memory_space=pl.ANY)
+    smem = pl.BlockSpec(memory_space=pltpu.SMEM)
     vmem = pl.BlockSpec(memory_space=pltpu.VMEM)
     n_out = max(NP - 1, 1)
     mixed, hg, gd, ug = pl.pallas_call(
@@ -349,16 +402,16 @@
         out_shape=(
             jax.ShapeDtypeStruct((cr, C), BF16),
             jax.ShapeDtypeStruct((hr, F), BF16),
-            jax.ShapeDtypeStruct((F, ndl), BF16),
+            jax.ShapeDtypeStruct((ndl, F), BF16),
             jax.ShapeDtypeStruct((nul, C), BF16),
         ),
-        in_specs=[anyspace, anyspace, anyspace, vmem, vmem, vmem, anyspace],
+        in_specs=[anyspace, anyspace, anyspace, vmem, smem, smem, anyspace],
         out_specs=(anyspace,) * 4,
         scratch_shapes=[
             pltpu.VMEM((F, C), BF16),
             pltpu.VMEM((J, hr, F), BF16),
             pltpu.VMEM((T, cr, C), BF16),
-            pltpu.VMEM((F, ndl), BF16),
+            pltpu.VMEM((ndl, F), BF16),
             pltpu.VMEM((NP, 2, hr, F), BF16),
             pltpu.VMEM((NP, hr, F), BF16),
             pltpu.VMEM((n_out, hr, F), BF16),
@@ -368,13 +421,15 @@
             pltpu.VMEM((nul, C), BF16),
             pltpu.VMEM((R, ndl), BF16),
             pltpu.VMEM((R, nul), BF16),
+            pltpu.VMEM((R, ndl), BF16),
+            pltpu.VMEM((R, nul), BF16),
             pltpu.VMEM((4, R // 2, 2 * RANK), BF16),
             pltpu.VMEM((T - 1, R // 2, 2 * RANK), BF16),
             pltpu.VMEM((J - 1, R // 2, 2 * RANK), BF16),
             pltpu.VMEM((T - 1, R // 2, 2 * RANK), BF16),
             pltpu.VMEM((J - 1, R // 2, 2 * RANK), BF16),
             sem((4,)),
-            sem((T - 1,)), sem((T - 1,)),
+            sem((2, T - 1)), sem((2, T - 1)),
             sem((1,)), sem((1,)),
             sem((n_out, chunks)), sem((n_out, chunks)),
             sem((n_out, chunks)), sem((n_out, chunks)),
@@ -388,8 +443,8 @@
         compiler_params=pltpu.CompilerParams(
             collective_id=0, has_side_effects=True, vmem_limit_bytes=64 * 1024 * 1024
         ),
-    )(hidden, weight, dn, up, mdn, mup, cotangent)
-    grad_down = jnp.transpose(gd.reshape(F, nd, RANK), (1, 0, 2))
+    )(hidden, weight, dn, up, block_jobs, home, cotangent)
+    grad_down = jnp.transpose(gd.reshape(nd, RANK, F), (0, 2, 1))
     return mixed, hg, grad_down, ug.reshape(nu, RANK, C)
 
 

time: 172 us -> 146 us (0.85)
  Pallas kernels: 156 us -> 137 us
  local copies, waits for them, and re-layouts: 12.3 us -> 7.05 us
  other arithmetic: 2.17 us -> 0 us
    pallas_call x1, Pallas kernels: 156 us -> 137 us  [per_device(): pl.pallas_call(functools.partial(step_kernel, T, J, ft, ct, chunks), out_...]
    unnamed x9 -> x8, local copies, waits for them, and re-layouts: 2.99 us -> 7.05 us
    pallas_call x1 -> x0, local copies, waits for them, and re-layouts: 4.03 us -> none  [per_device(): pl.pallas_call(functools.partial(step_kernel, T, J, ft, ct, chunks), out_...]
    reshape x1 -> x0, local copies, waits for them, and re-layouts: 3.87 us -> none  [per_device(): dn = jnp.transpose(downs, (1, 0, 2)).reshape(F, ndl)]
where the time goes in v2:
time: 146 us; the launch traced here: 145 us
  Pallas kernels  137 us (94%)
  local copies, waits for them, and re-layouts  7.05 us (5%)
    pallas_call x1, Pallas kernels, per_device(): pl.pallas_call(functools.partial(step_kernel, T, J, ft, ct, chunks), out_...  137 us
    unnamed x8, local copies, waits for them, and re-layouts  7.05 us

profile of v2, /device:TPU:25, one launch (start us, length us, event | category | flops | bytes accessed | tf_op | source)
XLA Modules:
  0.0 144.8 jit_solution(1441276998848057548)
XLA Ops:
  0.6 137.1 %shard_map.102 = (bf16[128,2048]{1,0:T(8,128)(2,1)}, bf16[128,7168]{1,0:T(8,128)(2,1)}, bf16[128,7168]{1,0:T(8,128)(2,1)}, bf16[128,2048]{1,0:T(8,128)(2,1)}) custom-call(bf16[128,7168]{1,0:T(8,128)(2,1)} %hid.1, bf16[7168,2048]{1,0:T(8,128)(2,1)} %w.1, bf16[128,7168]{1,0:T(8,128)(2,1)} %bitcast.9, bf16[128,2048]{1,0:T(8,128)(2,1)} %bitcast.10, s32[4]{0:T(128)} %ids.1, ...), custom_call_target="tpu_custom_call" | custom-call | tf_op jit(solution)/shard_map/pallas_call | solution.py:400
  137.8 1.9 %copy.15 = bf16[128,2048]{1,0:T(8,128)(2,1)} copy(bf16[128,2048]{1,0:T(8,128)(2,1)} %get-tuple-element.16) | data formatting | bytes 1048576
  139.7 0.0 copy-start
  139.7 3.0 %copy.16 = bf16[128,7168]{1,0:T(8,128)(2,1)} copy(bf16[128,7168]{1,0:T(8,128)(2,1)} %get-tuple-element.17) | data formatting | bytes 3670016
  142.7 0.0 copy-done
  142.7 0.0 copy-start.1
  142.7 1.2 copy.17
  143.9 0.2 copy-done.1
  144.1 0.8 copy.18
Async XLA Ops:
  139.7 3.0 %copy-start = (bf16[128,7168]{1,0:T(8,128)(2,1)S(1)}, bf16[128,7168]{1,0:T(8,128)(2,1)}, u32[]{:S(2)}) copy-start(bf16[128,7168]{1,0:T(8,128)(2,1)} %get-tuple-element.10) | copy-start | bytes 5505028
  142.7 1.4 copy-start.1

commit v3 on v2

--- a/solution.py
+++ b/solution.py
@@ -231,9 +231,21 @@
 
     blocks = 2 * hr // cr
 
-    def mixed_copy(d):
+    def mixed_copy(d, h):
         to = (t + d) % T
-        return to, remote(mst.at[to], mrv.at[d - 1], ms.at[d - 1], mr.at[d - 1], "tensor", to)
+        cols = pl.ds(h * (C // 2), C // 2)
+        return to, remote(
+            mst.at[to, :, cols], mrv.at[d - 1, :, cols],
+            ms.at[d - 1, h], mr.at[d - 1, h], "tensor", to,
+        )
+
+    def send_mixed(own, h):
+        for d in range(1, T):
+            to, copy = mixed_copy(d, h)
+
+            @pl.when((to // blocks == px) if own else (to // blocks != px))
+            def _():
+                copy.start()
 
     def pair_rows(pair):
         return pl.ds(pl.multiple_of(pair * 2 * hr, 2 * hr), 2 * hr)
@@ -282,7 +294,7 @@
                 blocks, cr, ct
             )
 
-    first = nft // 7
+    first = max(1, nft // 14)
     second = 2 * first
     pl.loop(0, first)(backward)
     pack[3] = total_of(pack.at[1], irj, inner_one).astype(BF16)
@@ -296,31 +308,21 @@
         value = fa[:, columns(n)] + nn_dot(innercat[pair_rows(px)], up[:, columns(n)])
         mst[pl.ds(px * blocks, blocks), :, columns(n)] = value.astype(BF16).reshape(blocks, cr, ct)
 
-    for d in range(1, T):
-        to, copy = mixed_copy(d)
-
-        @pl.when(to // blocks == px)
-        def _():
-            copy.start()
-
-    third = second
-    if nct <= nft - second:
-        third = second + nct
-
-        @pl.loop(0, nct)
-        def _(n):
-            other_forward(n)
+    send_mixed(True, 0)
+    send_mixed(True, 1)
+
+    beside = nct <= nft - second
+
+    def joint(n):
+        other_forward(n)
+        if beside:
             backward(second + n)
-    else:
-        pl.loop(0, nct)(other_forward)
-
-    for d in range(1, T):
-        to, copy = mixed_copy(d)
-
-        @pl.when(to // blocks != px)
-        def _():
-            copy.start()
-
+
+    pl.loop(0, nct // 2)(joint)
+    send_mixed(False, 0)
+    pl.loop(nct // 2, nct)(joint)
+    send_mixed(False, 1)
+    third = second + nct if beside else second
     pl.loop(third, nft)(backward)
     pass_on(nft - 1)
     out_gd = pltpu.make_async_copy(dnv, gd, outs.at[0])
@@ -345,15 +347,16 @@
     out_hg = pltpu.make_async_copy(bpb.at[px, c], hg, outs.at[2])
     out_hg.start()
 
-    for d in range(1, T):
-        mixed_copy(d)[1].wait_recv()
-
-    @pl.loop(0, nct)
-    def _(n):
-        value = mst[t, :, columns(n)].astype(F32)
+    for h in range(2):
         for d in range(1, T):
-            value = value + mrv[d - 1, :, columns(n)].astype(F32)
-        mst[t, :, columns(n)] = value.astype(BF16)
+            mixed_copy(d, h)[1].wait_recv()
+
+        @pl.loop(h * (nct // 2), (h + 1) * (nct // 2))
+        def _(n):
+            value = mst[t, :, columns(n)].astype(F32)
+            for d in range(1, T):
+                value = value + mrv[d - 1, :, columns(n)].astype(F32)
+            mst[t, :, columns(n)] = value.astype(BF16)
 
     out_mx = pltpu.make_async_copy(mst.at[t], mixed, outs.at[3])
     out_mx.start()
@@ -362,8 +365,9 @@
         copy.wait_send()
     for step in range(T - 1):
         line_each(step, lambda copy: copy.wait_send(), False)
-    for d in range(1, T):
-        mixed_copy(d)[1].wait_send()
+    for h in range(2):
+        for d in range(1, T):
+            mixed_copy(d, h)[1].wait_send()
 
     @pl.loop(0, nft)
     def _(k):
@@ -437,7 +441,7 @@
             sem((J - 1,)), sem((J - 1,)), sem((T - 1,)), sem((T - 1,)),
             sem((nft,)), sem((nft,)),
             sem((n_out, nft)), sem((n_out, nft)),
-            sem((T - 1,)), sem((T - 1,)),
+            sem((T - 1, 2)), sem((T - 1, 2)),
             sem((4,)),
         ],
         compiler_params=pltpu.CompilerParams(

time: 146 us -> 133 us (0.911)
  Pallas kernels: 137 us -> 123 us
    pallas_call x1, Pallas kernels: 137 us -> 123 us  [per_device(): pl.pallas_call(functools.partial(step_kernel, T, J, ft, ct, chunks), out_...]
where the time goes in v3:
time: 133 us; the launch traced here: 131 us
  Pallas kernels  123 us (92%)
  local copies, waits for them, and re-layouts  7.05 us (5%)
    pallas_call x1, Pallas kernels, per_device(): pl.pallas_call(functools.partial(step_kernel, T, J, ft, ct, chunks), out_...  123 us
    unnamed x8, local copies, waits for them, and re-layouts  7.05 us

profile of v3, /device:TPU:25, one launch (start us, length us, event | category | flops | bytes accessed | tf_op | source)
XLA Modules:
  0.0 130.8 jit_solution(129688889341130795)
XLA Ops:
  0.6 123.1 %shard_map.102 = (bf16[128,2048]{1,0:T(8,128)(2,1)}, bf16[128,7168]{1,0:T(8,128)(2,1)}, bf16[128,7168]{1,0:T(8,128)(2,1)}, bf16[128,2048]{1,0:T(8,128)(2,1)}) custom-call(bf16[128,7168]{1,0:T(8,128)(2,1)} %hid.1, bf16[7168,2048]{1,0:T(8,128)(2,1)} %w.1, bf16[128,7168]{1,0:T(8,128)(2,1)} %bitcast.9, bf16[128,2048]{1,0:T(8,128)(2,1)} %bitcast.10, s32[4]{0:T(128)} %ids.1, ...), custom_call_target="tpu_custom_call" | custom-call | tf_op jit(solution)/shard_map/pallas_call | solution.py:404
  123.7 1.9 %copy.15 = bf16[128,2048]{1,0:T(8,128)(2,1)} copy(bf16[128,2048]{1,0:T(8,128)(2,1)} %get-tuple-element.16) | data formatting | bytes 1048576
  125.6 0.0 copy-start
  125.6 3.0 %copy.16 = bf16[128,7168]{1,0:T(8,128)(2,1)} copy(bf16[128,7168]{1,0:T(8,128)(2,1)} %get-tuple-element.17) | data formatting | bytes 3670016
  128.6 0.0 copy-done
  128.6 0.0 copy-start.1
  128.6 1.2 copy.17
  129.8 0.2 copy-done.1
  130.0 0.8 copy.18
Async XLA Ops:
  125.6 3.0 %copy-start = (bf16[128,7168]{1,0:T(8,128)(2,1)S(1)}, bf16[128,7168]{1,0:T(8,128)(2,1)}, u32[]{:S(2)}) copy-start(bf16[128,7168]{1,0:T(8,128)(2,1)} %get-tuple-element.10) | copy-start | bytes 5505028
  128.6 1.4 %copy-start.1 = (bf16[128,2048]{1,0:T(8,128)(2,1)S(1)}, bf16[128,2048]{1,0:T(8,128)(2,1)}, u32[]{:S(2)}) copy-start(bf16[128,2048]{1,0:T(8,128)(2,1)} %get-tuple-element.11) | copy-start | bytes 1572868

commit v4 on v3

--- a/solution.py
+++ b/solution.py
@@ -233,7 +233,7 @@
 
     def mixed_copy(d, h):
         to = (t + d) % T
-        cols = pl.ds(h * (C // 2), C // 2)
+        cols = pl.ds(h * (C // 4), C // 4)
         return to, remote(
             mst.at[to, :, cols], mrv.at[d - 1, :, cols],
             ms.at[d - 1, h], mr.at[d - 1, h], "tensor", to,
@@ -308,8 +308,8 @@
         value = fa[:, columns(n)] + nn_dot(innercat[pair_rows(px)], up[:, columns(n)])
         mst[pl.ds(px * blocks, blocks), :, columns(n)] = value.astype(BF16).reshape(blocks, cr, ct)
 
-    send_mixed(True, 0)
-    send_mixed(True, 1)
+    for h in range(4):
+        send_mixed(True, h)
 
     beside = nct <= nft - second
 
@@ -318,10 +318,9 @@
         if beside:
             backward(second + n)
 
-    pl.loop(0, nct // 2)(joint)
-    send_mixed(False, 0)
-    pl.loop(nct // 2, nct)(joint)
-    send_mixed(False, 1)
+    for h in range(4):
+        pl.loop(h * (nct // 4), (h + 1) * (nct // 4))(joint)
+        send_mixed(False, h)
     third = second + nct if beside else second
     pl.loop(third, nft)(backward)
     pass_on(nft - 1)
@@ -347,11 +346,11 @@
     out_hg = pltpu.make_async_copy(bpb.at[px, c], hg, outs.at[2])
     out_hg.start()
 
-    for h in range(2):
+    for h in range(4):
         for d in range(1, T):
             mixed_copy(d, h)[1].wait_recv()
 
-        @pl.loop(h * (nct // 2), (h + 1) * (nct // 2))
+        @pl.loop(h * (nct // 4), (h + 1) * (nct // 4))
         def _(n):
             value = mst[t, :, columns(n)].astype(F32)
             for d in range(1, T):
@@ -365,7 +364,7 @@
         copy.wait_send()
     for step in range(T - 1):
         line_each(step, lambda copy: copy.wait_send(), False)
-    for h in range(2):
+    for h in range(4):
         for d in range(1, T):
             mixed_copy(d, h)[1].wait_send()
 
@@ -441,7 +440,7 @@
             sem((J - 1,)), sem((J - 1,)), sem((T - 1,)), sem((T - 1,)),
             sem((nft,)), sem((nft,)),
             sem((n_out, nft)), sem((n_out, nft)),
-            sem((T - 1, 2)), sem((T - 1, 2)),
+            sem((T - 1, 4)), sem((T - 1, 4)),
             sem((4,)),
         ],
         compiler_params=pltpu.CompilerParams(

time: 133 us -> 128 us (0.962)
  Pallas kernels: 123 us -> 119 us
    pallas_call x1, Pallas kernels: 123 us -> 119 us  [per_device(): pl.pallas_call(functools.partial(step_kernel, T, J, ft, ct, chunks), out_...]
where the time goes in v4:
time: 128 us; the launch traced here: 126 us
  Pallas kernels  119 us (93%)
  local copies, waits for them, and re-layouts  7.05 us (6%)
    pallas_call x1, Pallas kernels, per_device(): pl.pallas_call(functools.partial(step_kernel, T, J, ft, ct, chunks), out_...  119 us
    unnamed x8, local copies, waits for them, and re-layouts  7.05 us

profile of v4, /device:TPU:25, one launch (start us, length us, event | category | flops | bytes accessed | tf_op | source)
XLA Modules:
  0.0 126.2 jit_solution(2296523049011594790)
XLA Ops:
  0.6 118.5 %shard_map.102 = (bf16[128,2048]{1,0:T(8,128)(2,1)}, bf16[128,7168]{1,0:T(8,128)(2,1)}, bf16[128,7168]{1,0:T(8,128)(2,1)}, bf16[128,2048]{1,0:T(8,128)(2,1)}) custom-call(bf16[128,7168]{1,0:T(8,128)(2,1)} %hid.1, bf16[7168,2048]{1,0:T(8,128)(2,1)} %w.1, bf16[128,7168]{1,0:T(8,128)(2,1)} %bitcast.9, bf16[128,2048]{1,0:T(8,128)(2,1)} %bitcast.10, s32[4]{0:T(128)} %ids.1, ...), custom_call_target="tpu_custom_call" | custom-call | tf_op jit(solution)/shard_map/pallas_call | solution.py:403
  119.2 1.9 %copy.15 = bf16[128,2048]{1,0:T(8,128)(2,1)} copy(bf16[128,2048]{1,0:T(8,128)(2,1)} %get-tuple-element.16) | data formatting | bytes 1048576
  121.0 0.0 copy-start
  121.0 3.0 %copy.16 = bf16[128,7168]{1,0:T(8,128)(2,1)} copy(bf16[128,7168]{1,0:T(8,128)(2,1)} %get-tuple-element.17) | data formatting | bytes 3670016
  124.0 0.0 copy-done
  124.0 0.0 copy-start.1
  124.0 1.2 copy.17
  125.3 0.2 copy-done.1
  125.4 0.8 copy.18
Async XLA Ops:
  121.0 3.0 %copy-start = (bf16[128,7168]{1,0:T(8,128)(2,1)S(1)}, bf16[128,7168]{1,0:T(8,128)(2,1)}, u32[]{:S(2)}) copy-start(bf16[128,7168]{1,0:T(8,128)(2,1)} %get-tuple-element.10) | copy-start | bytes 5505028
  124.0 1.4 %copy-start.1 = (bf16[128,2048]{1,0:T(8,128)(2,1)S(1)}, bf16[128,2048]{1,0:T(8,128)(2,1)}, u32[]{:S(2)}) copy-start(bf16[128,2048]{1,0:T(8,128)(2,1)} %get-tuple-element.11) | copy-start | bytes 1572868
